TPU v7x, 32 devices: a whole 2x2x4 slice. The times are simulated.
32 devices in a mesh: tm: 16 (over z, x, core), quad: 2 (over y).
Axes of the slice: x: 2, y: 2, z: 4, core: 2. Of those that a mesh axis runs over, the one named last changes fastest.
Arguments:
- features: bfloat16 [16, 512, 192], P('tm', 'quad'), may hold values from -14 to 14
- w_query: bfloat16 [192, 192], replicated, may hold values from -1.25 to 1.25
- w_key: bfloat16 [192, 192], replicated, may hold values from -0.4375 to 0.4375
- w_value: bfloat16 [192, 192], replicated, may hold values from -0.4375 to 0.4375
- w_out: bfloat16 [192, 192], replicated, may hold values from -1.75 to 1.75
- block_offset: int32 [16, 4, 24], P('tm', 'quad'), may hold values from 0 to 2
- block_quad: int32 [16, 4, 24], P('tm', 'quad'), may hold values from 0 to 1
- block_tile: int32 [16, 4, 24], P('tm', 'quad'), may hold values from 0 to 1
- live_blocks: int32 [16, 4], P('tm', 'quad'), may hold values from 1 to 24, as said below
Outputs:
- mixed: bfloat16 [16, 512, 192], P('tm', 'quad')
Inputs may be any that keep to these rules, and one draw needn't show every extreme that they name: `live_blocks`: some device has every one of its query tiles at 24 live blocks; on a quarter of the devices or so all tiles are at 24.
All inputs are finite; a program needn't handle non-finite values.
Results may differ from a plain program's by a relative error of at most 0.008.
The roundings to bfloat16 on the way count: a program that leaves them out, or rounds other values in their place, can miss the bound.
Values may be sent and summed in bfloat16 or wider, within the bound.
A program may use at most 64 MiB of HBM per device.

v0:
```python
import jax
import jax.numpy as jnp
from jax import lax
from jax.sharding import PartitionSpec as P

HEADS = 6
TILE = 128
NB = 24
LOOP = 16


def shifted(block, axis, distance):
    devices = range(lax.axis_size(axis))
    route = [((i - distance) % len(devices), i) for i in devices]
    return lax.ppermute(block, axis, route)


def body(
    features, w_query, w_key, w_value, w_out, block_offset, block_quad, block_tile, live_blocks
):
    tokens = features[0]
    tok_count, width = tokens.shape
    head_dim = width // HEADS
    tiles = tok_count // TILE
    pieces = lax.axis_size("quad")
    stride = lax.axis_size("tm") // LOOP
    query = (
        jnp.dot(tokens, w_query, preferred_element_type=jnp.float32) * head_dim ** (-0.5)
    ).astype(jnp.bfloat16)
    keys = jnp.dot(tokens, w_key, preferred_element_type=jnp.float32).astype(jnp.bfloat16)
    values = jnp.dot(tokens, w_value, preferred_element_type=jnp.float32).astype(jnp.bfloat16)
    paired = jnp.stack([keys, values]).reshape(2, tiles, TILE * width)
    whole = lax.all_gather(paired, "quad", axis=1, tiled=True)
    earlier = shifted(whole, "tm", stride)
    later = shifted(whole, "tm", -stride)
    window = jnp.stack([earlier, whole, later], axis=1)
    window = window.reshape(2, 3 * pieces * tiles, TILE * width)
    block_ids = block_offset[0] * (pieces * tiles) + block_quad[0] * tiles + block_tile[0]
    query_tiles = query.reshape(tiles, TILE, width)
    counts = live_blocks[0]

    def attend(packed):
        qtile, ids, count = packed
        taken = jnp.take(window, ids, axis=1).reshape(2, NB * TILE, HEADS, head_dim)
        qheads = qtile.reshape(TILE, HEADS, head_dim)
        scores = jnp.einsum("qhd,khd->hqk", qheads, taken[0], preferred_element_type=jnp.float32)
        live = jnp.arange(NB * TILE, dtype=jnp.int32) // TILE < count
        scores = jnp.where(live[None, None, :], scores, -jnp.inf)
        top = jnp.max(scores, axis=-1, keepdims=True)
        weights = jnp.exp(scores - top)
        total = jnp.sum(weights, axis=-1)
        probs = weights.astype(jnp.bfloat16)
        summed = jnp.einsum("hqk,khd->qhd", probs, taken[1], preferred_element_type=jnp.float32)
        return (summed / total.T[:, :, None]).astype(jnp.bfloat16).reshape(TILE, width)

    attended = lax.map(attend, (query_tiles, block_ids, counts))
    mixed = jnp.dot(attended.reshape(tok_count, width), w_out, preferred_element_type=jnp.float32)
    return mixed.astype(jnp.bfloat16)[None]


def solution(mesh):
    return jax.shard_map(
        body,
        mesh=mesh,
        in_specs=(
            P("tm", "quad", None),
            P(),
            P(),
            P(),
            P(),
            P("tm", "quad", None),
            P("tm", "quad", None),
            P("tm", "quad", None),
            P("tm", "quad"),
        ),
        out_specs=P("tm", "quad", None),
        check_vma=False,
    )
```

profile of v0, /device:TPU:1, one launch (start us, length us, event | category | flops | bytes accessed | tf_op | source)
XLA Modules:
  0.0 132.9 jit_solution(17382061691464316859)
XLA Ops:
  0.0 0.9 copy-done
  0.9 1.1 convolution_convert_fusion.2
  2.3 1.1 convolution_convert_fusion.1
  4.2 7.4 %all_gather.3 = bf16[2,4,24576]{2,0,1:T(2,128)(2,1)S(1)} all-gather(bf16[2,2,24576]{2,0,1:T(2,128)(2,1)S(1)} %copy.24), channel_id=1, replica_groups=mesh['tm'=16,'quad'=2] {'quad'}, dimensions={1}, use_global_device_ids=true | all-gather | bytes 589824 | tf_op jit(solution)/shard_map/all_gather | solution.py:33
  11.6 2.6 %collective-permute-start = (bf16[2,4,24576]{2,0,1:T(2,128)(2,1)S(1)}, bf16[2,4,24576]{2,0,1:T(2,128)(2,1)S(1)}, u32[]{:S(2)}, u32[]{:S(2)}) collective-permute-start(bf16[2,4,24576]{2,0,1:T(2,128)(2,1)S(1)} %all_gather.3), channel_id=1, source_target_pairs={{30,0},{0,2},{2,4},{4,6},{6,8},{8,10},{10,12},{12,14},{14,16},{16,... | collective-permute-start | bytes 1179656 | tf_op jit(solution)/shard_map/ppermute | solution.py:15
  14.1 1.1 fusion.34
  15.3 0.7 add_bitcast_fusion
  16.0 7.1 %collective-permute-done = bf16[2,4,24576]{2,0,1:T(2,128)(2,1)S(1)} collective-permute-done((bf16[2,4,24576]{2,0,1:T(2,128)(2,1)S(1)}, bf16[2,4,24576]{2,0,1:T(2,128)(2,1)S(1)}, u32[]{:S(2)}, u32[]{:S(2)}) %collective-permute-start) | collective-permute-done | bytes 393248 | tf_op jit(solution)/shard_map/ppermute | solution.py:15
  23.1 2.5 %collective-permute-done.1 = bf16[2,4,24576]{2,0,1:T(2,128)(2,1)S(1)} collective-permute-done((bf16[2,4,24576]{2,0,1:T(2,128)(2,1)S(1)}, bf16[2,4,24576]{2,0,1:T(2,128)(2,1)S(1)}, u32[]{:S(2)}, u32[]{:S(2)}) %collective-permute-start.1) | collective-permute-done | bytes 393248 | tf_op jit(solution)/shard_map/ppermute | solution.py:15
  25.6 2.8 %pad_maximum_fusion = bf16[2,3,4,24576]{3,0,2,1:T(2,128)(2,1)} fusion(bf16[2,1,4,24576]{3,0,2,1:T(2,128)(2,1)S(1)} %bitcast.77, bf16[2,1,4,24576]{3,0,2,1:T(2,128)(2,1)S(1)} %bitcast.73, bf16[2,1,4,24576]{3,0,2,1:T(2,128)(2,1)S(1)} %bitcast.76), kind=kLoop, calls=%fused_computation.36 | loop fusion | flops 1179648 | bytes 2359296 | tf_op jit(solution)/shard_map/stack | solution.py:36
  28.4 103.7 %while.12 = (s32[]{:T(128)}, bf16[2,128,192]{1,2,0:T(8,128)(2,1)S(1)}, s32[2,24]{1,0:T(2,128)S(1)}, bf16[2,12,24576]{2,0,1:T(2,128)(2,1)}, s32[2]{0:T(128)S(1)}, /*index=5*/bf16[2,128,192]{1,2,0:T(8,128)(2,1)S(1)}, s32[]{:T(128)}) while((s32[]{:T(128)}, bf16[2,128,192]{1,2,0:T(8,128)(2,1)S(1)}, s32[2,24]{1,0:T(2,128)S(1)}, ...), condition=%wide.region_3.4_spmd, body=%wide.region_0.3_spmd.sunk | while | flops 322120416 | bytes 87621264 | solution.py:56
  28.4 8.8 %gather_fusion = bf16[24,2,24576]{2,1,0:T(2,128)(2,1)S(1)} fusion(bf16[2,12,24576]{2,0,1:T(2,128)(2,1)} %get-tuple-element.180, s32[1024]{0:T(1024)S(1)} %pad_clamp_fusion.2), kind=kCustom, calls=%fused_computation.clone.1 | custom fusion | bytes 4718688 | tf_op jit(solution)/shard_map/while/body/eval_jaxpr/jit(_take)/gather | solution.py:44
  37.2 2.1 %fusion.59 = bf16[2,24,24576]{2,0,1:T(2,128)(2,1)S(1)} fusion(bf16[24,2,24576]{2,1,0:T(2,128)(2,1)S(1)} %gather_fusion, pred[24]{0:T(512)(128)(4,1)S(1)} %compare_and_fusion.2), kind=kLoop, calls=%fused_computation.15.clone.1 | loop fusion | flops 1179648 | bytes 4718616 | tf_op jit(solution)/shard_map/while/body/eval_jaxpr/jit(_take)/select_n | solution.py:44
  39.4 10.4 %slice_reduce_fusion.3 = (bf16[24,24576]{1,0:T(8,128)(2,1)S(1)}, bf16[24,24576]{1,0:T(8,128)(2,1)S(1)}) fusion(bf16[2,24,24576]{2,0,1:T(2,128)(2,1)S(1)} %fusion.59), kind=kLoop, calls=%fused_computation.14.clone.1 | loop fusion | bytes 4718592 | tf_op jit(solution)/shard_map/while/body/eval_jaxpr/slice | solution.py:53
  49.8 6.6 %squeeze.40 = bf16[3072,6,32]{2,1,0:T(8,128)(2,1)} reshape(bf16[24,24576]{1,0:T(8,128)(2,1)S(1)} %get-tuple-element.159) | data formatting | bytes 2359296 | tf_op jit(solution)/shard_map/while/body/eval_jaxpr/squeeze | solution.py:46
  56.4 0.6 dynamic_slice.34
  57.6 4.6 %select_reduce_fusion.2 = (f32[6,128]{1,0:T(8,128)S(1)}, f32[6,128,3072]{2,1,0:T(8,128)S(1)}) fusion(pred[3072]{0:T(1024)(128)(4,1)S(1)} %fusion.57, bf16[128,6,32]{0,2,1:T(8,128)(2,1)S(1)} %bitcast.72, bf16[3072,6,32]{2,1,0:T(8,128)(2,1)} %squeeze.40), kind=kOutput, calls=%fused_computation.2.clone.1 | convolution fusion | flops 155712768 | bytes 10672128 | tf_op jit(solution)/shard_map/while/body/eval_jaxpr/qhd,khd->hqk/dot_general | solution.py:46
  62.2 1.8 %fusion.60 = f32[6,128]{1,0:T(8,128)S(1)} fusion(f32[6,128,3072]{2,1,0:T(8,128)S(1)} %get-tuple-element.160, f32[6,128]{1,0:T(8,128)S(1)} %get-tuple-element.161, pred[3072]{0:T(1024)(128)(4,1)S(1)} %fusion.57), kind=kLoop, calls=%fused_computation.3.clone.1 | loop fusion | flops 7077120 | bytes 9446400 | tf_op jit(solution)/shard_map/while/body/eval_jaxpr/reduce_sum | solution.py:51
  63.9 1.9 %copy-done.1 = f32[6,128,3072]{2,1,0:T(8,128)} copy-done((f32[6,128,3072]{2,1,0:T(8,128)}, f32[6,128,3072]{2,1,0:T(8,128)S(1)}, u32[]{:S(2)}) %copy-start.1) | copy-done | bytes 9437208 | tf_op jit(solution)/shard_map/while
  65.8 6.6 %squeeze.41 = bf16[3072,6,32]{2,1,0:T(8,128)(2,1)} reshape(bf16[24,24576]{1,0:T(8,128)(2,1)S(1)} %get-tuple-element.162) | data formatting | bytes 2359296 | tf_op jit(solution)/shard_map/while/body/eval_jaxpr/squeeze | solution.py:53
  72.4 7.8 %fusion.61 = bf16[128,6,32]{0,2,1:T(8,128)(2,1)S(1)} fusion(f32[6,128,3072]{2,1,0:T(8,128)} %copy-done.1, f32[6,128]{1,0:T(8,128)S(1)} %get-tuple-element.161, pred[3072]{0:T(1024)(128)(4,1)S(1)} %fusion.57, bf16[3072,6,32]{2,1,0:T(8,128)(2,1)} %squeeze.41, f32[128,6]{0,1:T(8,128)S(1)} %bitcast.78), kind=kOutput, calls=%fused_computation.18.clone.1 | convolution fusion | flops 158121984 | bytes 10675200 | tf_op jit(solution)/shard_map/while/body/eval_jaxpr/hqk,khd->qhd/dot_general | solution.py:53
  80.2 8.8 %gather_fusion = bf16[24,2,24576]{2,1,0:T(2,128)(2,1)S(1)} fusion(bf16[2,12,24576]{2,0,1:T(2,128)(2,1)} %get-tuple-element.180, s32[1024]{0:T(1024)S(1)} %pad_clamp_fusion.2), kind=kCustom, calls=%fused_computation.clone.1 | custom fusion | bytes 4718688 | tf_op jit(solution)/shard_map/while/body/eval_jaxpr/jit(_take)/gather | solution.py:44
  89.1 2.1 %fusion.59 = bf16[2,24,24576]{2,0,1:T(2,128)(2,1)S(1)} fusion(bf16[24,2,24576]{2,1,0:T(2,128)(2,1)S(1)} %gather_fusion, pred[24]{0:T(512)(128)(4,1)S(1)} %compare_and_fusion.2), kind=kLoop, calls=%fused_computation.15.clone.1 | loop fusion | flops 1179648 | bytes 4718616 | tf_op jit(solution)/shard_map/while/body/eval_jaxpr/jit(_take)/select_n | solution.py:44
  91.2 10.4 %slice_reduce_fusion.3 = (bf16[24,24576]{1,0:T(8,128)(2,1)S(1)}, bf16[24,24576]{1,0:T(8,128)(2,1)S(1)}) fusion(bf16[2,24,24576]{2,0,1:T(2,128)(2,1)S(1)} %fusion.59), kind=kLoop, calls=%fused_computation.14.clone.1 | loop fusion | bytes 4718592 | tf_op jit(solution)/shard_map/while/body/eval_jaxpr/slice | solution.py:53
  101.6 6.6 %squeeze.40 = bf16[3072,6,32]{2,1,0:T(8,128)(2,1)} reshape(bf16[24,24576]{1,0:T(8,128)(2,1)S(1)} %get-tuple-element.159) | data formatting | bytes 2359296 | tf_op jit(solution)/shard_map/while/body/eval_jaxpr/squeeze | solution.py:46
  108.2 0.6 dynamic_slice.34
  109.4 4.6 %select_reduce_fusion.2 = (f32[6,128]{1,0:T(8,128)S(1)}, f32[6,128,3072]{2,1,0:T(8,128)S(1)}) fusion(pred[3072]{0:T(1024)(128)(4,1)S(1)} %fusion.57, bf16[128,6,32]{0,2,1:T(8,128)(2,1)S(1)} %bitcast.72, bf16[3072,6,32]{2,1,0:T(8,128)(2,1)} %squeeze.40), kind=kOutput, calls=%fused_computation.2.clone.1 | convolution fusion | flops 155712768 | bytes 10672128 | tf_op jit(solution)/shard_map/while/body/eval_jaxpr/qhd,khd->hqk/dot_general | solution.py:46
  114.0 1.8 %fusion.60 = f32[6,128]{1,0:T(8,128)S(1)} fusion(f32[6,128,3072]{2,1,0:T(8,128)S(1)} %get-tuple-element.160, f32[6,128]{1,0:T(8,128)S(1)} %get-tuple-element.161, pred[3072]{0:T(1024)(128)(4,1)S(1)} %fusion.57), kind=kLoop, calls=%fused_computation.3.clone.1 | loop fusion | flops 7077120 | bytes 9446400 | tf_op jit(solution)/shard_map/while/body/eval_jaxpr/reduce_sum | solution.py:51
  115.8 1.9 %copy-done.1 = f32[6,128,3072]{2,1,0:T(8,128)} copy-done((f32[6,128,3072]{2,1,0:T(8,128)}, f32[6,128,3072]{2,1,0:T(8,128)S(1)}, u32[]{:S(2)}) %copy-start.1) | copy-done | bytes 9437208 | tf_op jit(solution)/shard_map/while
  117.6 6.6 %squeeze.41 = bf16[3072,6,32]{2,1,0:T(8,128)(2,1)} reshape(bf16[24,24576]{1,0:T(8,128)(2,1)S(1)} %get-tuple-element.162) | data formatting | bytes 2359296 | tf_op jit(solution)/shard_map/while/body/eval_jaxpr/squeeze | solution.py:53
  124.2 7.8 %fusion.61 = bf16[128,6,32]{0,2,1:T(8,128)(2,1)S(1)} fusion(f32[6,128,3072]{2,1,0:T(8,128)} %copy-done.1, f32[6,128]{1,0:T(8,128)S(1)} %get-tuple-element.161, pred[3072]{0:T(1024)(128)(4,1)S(1)} %fusion.57, bf16[3072,6,32]{2,1,0:T(8,128)(2,1)} %squeeze.41, f32[128,6]{0,1:T(8,128)S(1)} %bitcast.78), kind=kOutput, calls=%fused_computation.18.clone.1 | convolution fusion | flops 158121984 | bytes 10675200 | tf_op jit(solution)/shard_map/while/body/eval_jaxpr/hqk,khd->qhd/dot_general | solution.py:53
  132.1 0.9 fusion.33
  (28 shorter events, 2.3 us)
Async XLA Ops:
  0.0 0.9 copy-start
  0.0 28.3 %copy-start.3 = (s32[1,2]{1,0:T(1,128)S(1)}, s32[1,2]{1,0:T(1,128)}, u32[]{:S(2)}) copy-start(s32[1,2]{1,0:T(1,128)} %param.19) | copy-start | bytes 28
  11.6 11.5 %collective-permute-start = (bf16[2,4,24576]{2,0,1:T(2,128)(2,1)S(1)}, bf16[2,4,24576]{2,0,1:T(2,128)(2,1)S(1)}, u32[]{:S(2)}, u32[]{:S(2)}) collective-permute-start(bf16[2,4,24576]{2,0,1:T(2,128)(2,1)S(1)} %all_gather.3), channel_id=1, source_target_pairs={{30,0},{0,2},{2,4},{4,6},{6,8},{8,10},{10,12},{12,14},{14,16},{16,... | collective-permute-start | bytes 1179656 | tf_op jit(solution)/shard_map/ppermute | solution.py:15
  14.1 11.4 %collective-permute-start.1 = (bf16[2,4,24576]{2,0,1:T(2,128)(2,1)S(1)}, bf16[2,4,24576]{2,0,1:T(2,128)(2,1)S(1)}, u32[]{:S(2)}, u32[]{:S(2)}) collective-permute-start(bf16[2,4,24576]{2,0,1:T(2,128)(2,1)S(1)} %all_gather.3), channel_id=1, source_target_pairs={{2,0},{4,2},{6,4},{8,6},{10,8},{12,10},{14,12},{16,14},{18,16},{20... | collective-permute-start | bytes 1179656 | tf_op jit(solution)/shard_map/ppermute | solution.py:15
  28.3 103.7 %copy-start.2 = (bf16[192,192]{1,0:T(8,128)(2,1)S(1)}, bf16[192,192]{1,0:T(8,128)(2,1)}, u32[]{:S(2)}) copy-start(bf16[192,192]{1,0:T(8,128)(2,1)} %param.15) | copy-start | bytes 221188
  62.2 3.6 %copy-start.1 = (f32[6,128,3072]{2,1,0:T(8,128)}, f32[6,128,3072]{2,1,0:T(8,128)S(1)}, u32[]{:S(2)}) copy-start(f32[6,128,3072]{2,1,0:T(8,128)S(1)} %get-tuple-element.160) | copy-start | bytes 28311556 | tf_op jit(solution)/shard_map/while
  114.0 3.6 %copy-start.1 = (f32[6,128,3072]{2,1,0:T(8,128)}, f32[6,128,3072]{2,1,0:T(8,128)S(1)}, u32[]{:S(2)}) copy-start(f32[6,128,3072]{2,1,0:T(8,128)S(1)} %get-tuple-element.160) | copy-start | bytes 28311556 | tf_op jit(solution)/shard_map/while
where the time goes:
time: 133 us
  local copies, waits for them, and re-layouts  71.4 us (54%)
  matrix products  29 us (22%)
  other arithmetic  12.8 us (10%)
  waiting for transfers between devices  9.55 us (7%)
  blocking collectives  7.35 us (6%)
  starting transfers between devices  2.57 us (2%)
    slice x2, local copies, waits for them, and re-layouts, attend(): taken[1]  20.8 us
    gather x2, local copies, waits for them, and re-layouts, attend(): taken = jnp.take(window, ids, axis=1).reshape(2, NB * TILE, HEADS, head_dim)  17.6 us
    dot_general x2, matrix products, attend(): jnp.einsum('hqk,khd->qhd', probs, taken[1], preferred_element_type=jnp.fl...  15.6 us
    squeeze x2, local copies, waits for them, and re-layouts, attend(): taken[0]  13.3 us
    squeeze x2, local copies, waits for them, and re-layouts, attend(): taken[1]  13.2 us
    ppermute x2, waiting for transfers between devices, shifted(): return lax.ppermute(block, axis, route)  9.55 us
    dot_general x2, matrix products, attend(): jnp.einsum('qhd,khd->hqk', qheads, taken[0], preferred_element_type=jnp.f...  9.17 us
    all_gather x1, blocking collectives, body(): whole = lax.all_gather(paired, 'quad', axis=1, tiled=True)  7.35 us
  transfers between devices with their start and end apart: 2, of which 2 were waited for; matrix products, arithmetic and copies ran while one was open for 1% of the time, Pallas kernels for 0%

commit v1 on v0

v1 whole, which is shorter than its diff:
```python
import functools

import jax
import jax.numpy as jnp
from jax import lax
from jax.experimental import pallas as pl
from jax.experimental.pallas import tpu as pltpu
from jax.sharding import PartitionSpec as P

HEADS = 6
TILE = 128
LOOP = 16
PARTS = 3
DEAD = -1e30
MESH = pl.DeviceIdType.MESH


def dot(a, b):
    return jnp.dot(a, b, preferred_element_type=jnp.float32)


def dot_nt(a, b):
    return lax.dot_general(a, b, (((1,), (1,)), ((), ())), preferred_element_type=jnp.float32)


def lanes(rows, columns):
    return lax.broadcasted_iota(jnp.int32, (rows, columns), 1)


def sublanes(rows, columns):
    return lax.broadcasted_iota(jnp.int32, (rows, columns), 0)


def kernel(
    pieces, frames, stride,
    feat_ref, wq_ref, wk_ref, wv_ref, offset_ref, quad_ref, tile_ref, live_ref,
    out_ref,
    window, wq, wk, wv, heads_q, bias, scores, peak, values, probs,
    load_sem, send_sem, recv_sem,
):
    tok, width = feat_ref.shape[1:]
    wide = heads_q.shape[-1]
    head_dim = width // HEADS
    tiles = tok // TILE
    frame, quad = lax.axis_index("tm"), lax.axis_index("quad")
    near, far = 2 - 2 * lax.rem(frame, 2), 2 * lax.rem(frame, 2)

    peers = []
    for rank, which in enumerate((far, 1, near)):
        for turn in range(pieces):
            if rank == 1 and turn == 0:
                continue
            there = lax.rem(frame + (which - 1) * stride + frames, frames)
            slot = (2 - which) * pieces + quad
            peers.append(({"tm": there, "quad": lax.rem(quad + turn, pieces)}, slot))

    barrier = pltpu.get_barrier_semaphore()
    for device, _ in peers:
        pl.semaphore_signal(barrier, inc=1, device_id=device, device_id_type=MESH)

    own = pieces + quad
    loads = [
        pltpu.make_async_copy(source, target, load_sem.at[n])
        for n, (source, target) in enumerate(
            ((feat_ref.at[0], window.at[own]), (wq_ref, wq), (wk_ref, wk), (wv_ref, wv))
        )
    ]
    for load in loads:
        load.start()
    pl.semaphore_wait(barrier, len(peers))
    sends = []
    for n, (device, slot) in enumerate(peers):
        send = pltpu.make_async_remote_copy(
            src_ref=feat_ref.at[0],
            dst_ref=window.at[slot],
            send_sem=send_sem.at[n],
            recv_sem=recv_sem.at[slot],
            device_id=device,
            device_id_type=MESH,
        )
        send.start()
        sends.append(send)

    rows = bias.shape[0]
    ids = offset_ref[0] * (pieces * tiles) + quad_ref[0] * tiles + tile_ref[0]
    blocks = ids.shape[1]
    lane = lanes(rows, wide)
    table = jnp.zeros((rows, wide), jnp.float32)
    for t in range(tiles):
        hit = (ids[t : t + 1] == sublanes(rows, blocks)) & (
            lanes(rows, blocks) < live_ref[:, t : t + 1]
        )
        count = jnp.sum(hit.astype(jnp.float32), axis=1, keepdims=True)
        rest = jnp.where(count > 0, jnp.log(jnp.maximum(count, 1.0)), DEAD)
        for part in range(PARTS):
            piece = rest.astype(jnp.bfloat16).astype(jnp.float32)
            table = table + jnp.where(lane == width + t * PARTS + part, piece, 0.0)
            rest = jnp.where(count > 0, rest - piece, 0.0)
    bias[...] = table
    peak[...] = jnp.full(peak.shape, -jnp.inf, jnp.float32)

    for load in loads:
        load.wait()
    place = (sublanes(width, wide) == lanes(width, wide)).astype(jnp.bfloat16)
    wide_q = dot(wq[...], place).astype(jnp.bfloat16)
    wide_k = dot(wk[...], place).astype(jnp.bfloat16)
    wide_v = dot(wv[...], place).astype(jnp.bfloat16)

    lane = lanes(tok, wide)
    query = (dot(window[own], wide_q) * head_dim ** (-0.5)).astype(jnp.bfloat16).astype(jnp.float32)
    row_tile = sublanes(tok, wide) // TILE
    start = width + row_tile * PARTS
    pick = ((lane >= start) & (lane < start + PARTS)).astype(jnp.float32)
    for h in range(HEADS):
        mine = (lane >= h * head_dim) & (lane < (h + 1) * head_dim)
        heads_q[h] = jnp.where(mine, query, pick).astype(jnp.bfloat16)
    ones = (lane >= width).astype(jnp.float32)

    def gather(step, slot):
        x = window[slot]
        column = pl.ds(pl.multiple_of(step * tok, tok), tok)
        keys = dot(x, wide_k)
        keys = jnp.concatenate(
            [
                keys[t * TILE : (t + 1) * TILE] + bias[pl.ds(slot * tiles + t, 1), :]
                for t in range(tiles)
            ],
            axis=0,
        ).astype(jnp.bfloat16)
        values[column, :] = (dot(x, wide_v) + ones).astype(jnp.bfloat16)
        for h in range(HEADS):
            s = dot_nt(heads_q[h], keys)
            scores[h, :, column] = s
            top = peak[h]
            for c in range(0, tok, TILE):
                top = jnp.maximum(top, s[:, c : c + TILE])
            peak[h] = top

    gather(0, own)

    def arrive(step, carry):
        turn = step // pieces
        which = jnp.where(turn == 0, 1, jnp.where(turn == 1, near, far))
        slot = which * pieces + lax.rem(quad + lax.rem(step, pieces), pieces)
        pltpu.make_async_copy(feat_ref.at[0], window.at[slot], recv_sem.at[slot]).wait()
        gather(step, slot)
        return carry

    lax.fori_loop(1, 3 * pieces, arrive, 0)

    keys_all = values.shape[0]
    total = jnp.zeros((tok, wide), jnp.float32)
    summed = jnp.zeros((tok, wide), jnp.float32)
    for h in range(HEADS):
        top = jnp.max(peak[h], axis=1, keepdims=True)
        for c in range(0, keys_all, tok):
            probs[h % 2, :, c : c + tok] = jnp.exp(scores[h, :, c : c + tok] - top).astype(jnp.bfloat16)
        o = dot(probs[h % 2], values[...])
        mine = (lane >= h * head_dim) & (lane < (h + 1) * head_dim)
        total = jnp.where(mine, o[:, width : width + 1], total)
        summed = jnp.where(mine, o, summed)
    out_ref[...] = (summed[:, :width] / total[:, :width]).astype(jnp.bfloat16)
    for send in sends:
        send.wait_send()


def body(
    features, w_query, w_key, w_value, w_out, block_offset, block_quad, block_tile, live_blocks
):
    tok, width = features.shape[1:]
    tiles = tok // TILE
    pieces, frames = lax.axis_size("quad"), lax.axis_size("tm")
    stride = frames // LOOP
    slots = 3 * pieces
    wide = -(-(width + PARTS * tiles) // 128) * 128
    keys = slots * tok
    rows = -(-slots * tiles // 8) * 8
    hbm = pl.BlockSpec(memory_space=pl.ANY)
    vmem = pl.BlockSpec(memory_space=pltpu.VMEM)
    big = HEADS * tok * keys * 4 + keys * wide * 2 + 2 * tok * keys * 2 + slots * tok * wide * 2
    attended = pl.pallas_call(
        functools.partial(kernel, pieces, frames, stride),
        out_shape=jax.ShapeDtypeStruct((tok, width), jnp.bfloat16),
        in_specs=[hbm] * 4 + [vmem] * 4,
        out_specs=vmem,
        scratch_shapes=[
            pltpu.VMEM((slots, tok, width), jnp.bfloat16),
            pltpu.VMEM((width, width), jnp.bfloat16),
            pltpu.VMEM((width, width), jnp.bfloat16),
            pltpu.VMEM((width, width), jnp.bfloat16),
            pltpu.VMEM((HEADS, tok, wide), jnp.bfloat16),
            pltpu.VMEM((rows, wide), jnp.float32),
            pltpu.VMEM((HEADS, tok, keys), jnp.float32),
            pltpu.VMEM((HEADS, tok, TILE), jnp.float32),
            pltpu.VMEM((keys, wide), jnp.bfloat16),
            pltpu.VMEM((2, tok, keys), jnp.bfloat16),
            pltpu.SemaphoreType.DMA((4,)),
            pltpu.SemaphoreType.DMA((slots - 1,)),
            pltpu.SemaphoreType.DMA((slots,)),
        ],
        compiler_params=pltpu.CompilerParams(
            collective_id=0, has_side_effects=True, vmem_limit_bytes=big + (8 << 20)
        ),
    )(features, w_query, w_key, w_value, block_offset, block_quad, block_tile, live_blocks)
    return jnp.dot(attended, w_out, preferred_element_type=jnp.float32).astype(jnp.bfloat16)[None]


def solution(mesh):
    listed = P("tm", "quad", None)
    return jax.shard_map(
        body,
        mesh=mesh,
        in_specs=(listed, P(), P(), P(), P(), listed, listed, listed, P("tm", "quad")),
        out_specs=listed,
        check_vma=False,
    )
```

time: 133 us -> 20.2 us (0.15)
  the two profiles are of different devices: /device:TPU:1 before, /device:TPU:0 now
where the time goes in v1:
time: 20.2 us; the launch traced here: 20 us
  Pallas kernels  17 us (84%)
  local copies, waits for them, and re-layouts  2.01 us (10%)
  matrix products  0.88 us (4%)
    pallas_call x1, Pallas kernels, body(): pl.pallas_call(functools.partial(kernel, pieces, frames, stride), out_sha...  17 us
    unnamed x17, local copies, waits for them, and re-layouts  2.01 us
    dot_general x1, matrix products, body(): jnp.dot(attended, w_out, preferred_element_type=jnp.float32)  0.88 us

profile of v1, /device:TPU:0, one launch (start us, length us, event | category | flops | bytes accessed | tf_op | source)
XLA Modules:
  0.0 20.0 jit_solution(6827815399908089054)
XLA Ops:
  0.0 0.0 copy-start
  0.0 0.0 copy-start.7
  0.0 0.0 copy-start.6
  0.0 0.0 copy-start.5
  0.0 0.0 copy-start.4
  0.0 0.0 copy-start.2
  0.0 0.0 copy-start.1
  0.0 1.1 %copy.10.feat_ref = bf16[1,256,192]{2,1,0:T(8,128)(2,1)S(1)} copy(bf16[1,256,192]{1,2,0:T(8,128)(2,1)} %param.9) | data formatting | bytes 196608 | tf_op args[0]
  1.1 0.0 copy-done.7
  1.2 0.0 copy-done.6
  1.2 0.0 copy-done.5
  1.2 0.0 copy-done.4
  1.2 0.0 copy-done.2
  1.2 0.0 copy-done.1
  1.2 0.0 copy-start.3
  1.2 0.9 %copy-done.3 = bf16[192,192]{1,0:T(8,128)(2,1)S(1)} copy-done((bf16[192,192]{1,0:T(8,128)(2,1)S(1)}, bf16[192,192]{1,0:T(8,128)(2,1)}, u32[]{:S(2)}) %copy-start.3) | copy-done | bytes 73752
  2.1 17.0 %shard_map.91 = bf16[256,192]{1,0:T(8,128)(2,1)S(1)} custom-call(bf16[1,256,192]{2,1,0:T(8,128)(2,1)S(1)} %copy.10.feat_ref, bf16[192,192]{1,0:T(8,128)(2,1)S(1)} %copy-done.1, bf16[192,192]{1,0:T(8,128)(2,1)S(1)} %copy-done.2, bf16[192,192]{1,0:T(8,128)(2,1)S(1)} %copy-done.3, s32[1,2,24]{2,1,0:T(2,128)S(1)} %copy-done.4, s32[1,2,24]{2,1,0:T(2,128)S(1)} %copy-done.5, ...), custom_call_target="tpu_custom_call" | custom-call | tf_op jit(solution)/shard_map/pallas_call | solution.py:181
  19.1 0.0 copy-done
  19.2 0.9 %fusion = bf16[1,256,192]{1,2,0:T(8,128)(2,1)} fusion(bf16[256,192]{1,0:T(8,128)(2,1)S(1)} %shard_map.91, bf16[192,192]{1,0:T(8,128)(2,1)S(1)} %copy-done), kind=kOutput, calls=%fused_computation.1 | convolution fusion | flops 18923520 | bytes 270336 | tf_op jit(solution)/shard_map/dot_general | solution.py:205
Async XLA Ops:
  0.0 19.1 %copy-start = (bf16[192,192]{1,0:T(8,128)(2,1)S(1)}, bf16[192,192]{1,0:T(8,128)(2,1)}, u32[]{:S(2)}) copy-start(bf16[192,192]{1,0:T(8,128)(2,1)} %param.13) | copy-start | bytes 221188
  0.0 1.1 %copy-start.7 = (s32[1,2]{1,0:T(1,128)S(1)}, s32[1,2]{1,0:T(1,128)}, u32[]{:S(2)}) copy-start(s32[1,2]{1,0:T(1,128)} %live_ref.1) | copy-start | bytes 28
  0.0 1.2 %copy-start.6 = (s32[1,2,24]{2,1,0:T(2,128)S(1)}, s32[1,2,24]{2,1,0:T(2,128)}, u32[]{:S(2)}) copy-start(s32[1,2,24]{2,1,0:T(2,128)} %tile_ref.1) | copy-start | bytes 580
  0.0 1.2 %copy-start.5 = (s32[1,2,24]{2,1,0:T(2,128)S(1)}, s32[1,2,24]{2,1,0:T(2,128)}, u32[]{:S(2)}) copy-start(s32[1,2,24]{2,1,0:T(2,128)} %quad_ref.1) | copy-start | bytes 580
  0.0 1.2 %copy-start.4 = (s32[1,2,24]{2,1,0:T(2,128)S(1)}, s32[1,2,24]{2,1,0:T(2,128)}, u32[]{:S(2)}) copy-start(s32[1,2,24]{2,1,0:T(2,128)} %offset_ref.1) | copy-start | bytes 580
  0.0 1.2 %copy-start.2 = (bf16[192,192]{1,0:T(8,128)(2,1)S(1)}, bf16[192,192]{1,0:T(8,128)(2,1)}, u32[]{:S(2)}) copy-start(bf16[192,192]{1,0:T(8,128)(2,1)} %wk_ref.1) | copy-start | bytes 221188
  0.0 1.2 %copy-start.1 = (bf16[192,192]{1,0:T(8,128)(2,1)S(1)}, bf16[192,192]{1,0:T(8,128)(2,1)}, u32[]{:S(2)}) copy-start(bf16[192,192]{1,0:T(8,128)(2,1)} %wq_ref.1) | copy-start | bytes 221188
  1.2 0.9 %copy-start.3 = (bf16[192,192]{1,0:T(8,128)(2,1)S(1)}, bf16[192,192]{1,0:T(8,128)(2,1)}, u32[]{:S(2)}) copy-start(bf16[192,192]{1,0:T(8,128)(2,1)} %wv_ref.1) | copy-start | bytes 221188

commit v2 on v1

v2 whole, which is shorter than its diff:
```python
import functools

import jax
import jax.numpy as jnp
from jax import lax
from jax.experimental import pallas as pl
from jax.experimental.pallas import tpu as pltpu
from jax.sharding import PartitionSpec as P

HEADS = 6
TILE = 128
LOOP = 16
FAR = 1e30
MESH = pl.DeviceIdType.MESH


def dot(a, b):
    return jnp.dot(a, b, preferred_element_type=jnp.float32)


def lanes(rows, columns):
    return lax.broadcasted_iota(jnp.int32, (rows, columns), 1)


def sublanes(rows, columns):
    return lax.broadcasted_iota(jnp.int32, (rows, columns), 0)


def kernel(
    pieces, frames, stride,
    feat_ref, wq_ref, wk_ref, wv_ref, offset_ref, quad_ref, tile_ref, live_ref,
    out_ref,
    window, wq, wk, wv, offset, quads, places, live,
    queries, times, scores, peak, values,
    load_sem, send_sem, recv_sem,
):
    width, tok = feat_ref.shape
    head_dim = width // HEADS
    tiles = tok // TILE
    slots = 3 * pieces
    frame, quad = lax.axis_index("tm"), lax.axis_index("quad")
    near, far = 2 - 2 * lax.rem(frame, 2), 2 * lax.rem(frame, 2)
    own = pieces + quad

    peers = []
    for rank, which in enumerate((far, 1, near)):
        for turn in range(pieces):
            if rank == 1 and turn == 0:
                continue
            there = lax.rem(frame + (which - 1) * stride + frames, frames)
            slot = (2 - which) * pieces + quad
            peers.append(({"tm": there, "quad": lax.rem(quad + turn, pieces)}, slot))

    barrier = pltpu.get_barrier_semaphore()
    for device, _ in peers:
        pl.semaphore_signal(barrier, inc=1, device_id=device, device_id_type=MESH)

    pairs = (
        (wq_ref, wq), (feat_ref, window.at[own]), (wk_ref, wk), (wv_ref, wv),
        (offset_ref, offset), (quad_ref, quads), (tile_ref, places), (live_ref, live),
    )
    loads = [
        pltpu.make_async_copy(source, target, load_sem.at[n])
        for n, (source, target) in enumerate(pairs)
    ]
    for load in loads:
        load.start()
    pl.semaphore_wait(barrier, len(peers))
    sends = []
    for n, (device, slot) in enumerate(peers):
        send = pltpu.make_async_remote_copy(
            src_ref=feat_ref,
            dst_ref=window.at[slot],
            send_sem=send_sem.at[n],
            recv_sem=recv_sem.at[slot],
            device_id=device,
            device_id_type=MESH,
        )
        send.start()
        sends.append(send)
    for load in loads:
        load.wait()

    rows = times.shape[0]
    ids = offset[0] * (pieces * tiles) + quads[0] * tiles + places[0]
    blocks = ids.shape[1]
    query_tile = lanes(rows, tok) // TILE
    table = jnp.zeros((rows, tok), jnp.float32)
    for t in range(tiles):
        hit = (ids[t : t + 1] == sublanes(rows, blocks)) & (
            lanes(rows, blocks) < live[:, t : t + 1]
        )
        count = jnp.sum(hit.astype(jnp.float32), axis=1, keepdims=True)
        table = jnp.where(query_tile == t, count, table)
    times[...] = table
    peak[...] = jnp.full(peak.shape, -jnp.inf, jnp.float32)

    turned_q, turned_v = wq[...].T, wv[...].T
    query = (dot(turned_q, window[own]) * head_dim ** (-0.5)).astype(jnp.bfloat16)
    head = sublanes(width, tok) // head_dim
    for h in range(HEADS):
        queries[h] = jnp.where(head == h, query, jnp.zeros_like(query))
    key_tile = lanes(width, tok) // TILE

    def gather(slot):
        x = window[slot]
        keys = dot(x.T, wk[...]).astype(jnp.bfloat16)
        value = dot(turned_v, x).astype(jnp.bfloat16)
        for j in range(tiles):
            values[slot, j] = jnp.where(key_tile == j, value, jnp.zeros_like(value))
        used = [times[pl.ds(slot * tiles + j, 1), :] > 0 for j in range(tiles)]
        for h in range(HEADS):
            s = dot(keys, queries[h])
            scores[slot, h] = s
            top = peak[h]
            for j in range(tiles):
                part = s[j * TILE : (j + 1) * TILE].reshape(TILE // 8, 8, tok).max(axis=0)
                top = jnp.maximum(top, jnp.where(used[j], part, -jnp.inf))
            peak[h] = top

    gather(own)

    def arrive(step, carry):
        turn = step // pieces
        which = jnp.where(turn == 0, 1, jnp.where(turn == 1, near, far))
        slot = which * pieces + lax.rem(quad + lax.rem(step, pieces), pieces)
        pltpu.make_async_copy(feat_ref, window.at[slot], recv_sem.at[slot]).wait()
        gather(slot)
        return carry

    lax.fori_loop(1, slots, arrive, 0)

    for h in range(HEADS):
        top = jnp.max(peak[h], axis=0, keepdims=True)
        total = jnp.zeros((8, tok), jnp.float32)
        summed = jnp.zeros((head_dim, tok), jnp.float32)
        span = slice(h * head_dim, (h + 1) * head_dim)
        for slot in range(slots):
            probs, often = [], []
            for j in range(tiles):
                u = slot * tiles + j
                many = times[u : u + 1, :]
                shift = jnp.where(many > 0, top, FAR)
                w = jnp.exp(scores[slot, h, j * TILE : (j + 1) * TILE] - shift)
                total = total + many * w.reshape(TILE // 8, 8, tok).sum(axis=0)
                probs.append(w.astype(jnp.bfloat16))
                often.append(many)
            left = jnp.concatenate([values[slot, j, span] for j in range(tiles)], axis=0)
            o = dot(left, jnp.concatenate(probs, axis=0))
            for j in range(tiles):
                summed = summed + often[j] * o[j * head_dim : (j + 1) * head_dim]
        total = jnp.sum(total, axis=0, keepdims=True)
        out_ref[span, :] = (summed / total).astype(jnp.bfloat16)
    for send in sends:
        send.wait_send()


def body(
    features, w_query, w_key, w_value, w_out, block_offset, block_quad, block_tile, live_blocks
):
    tok, width = features.shape[1:]
    tiles = tok // TILE
    pieces, frames = lax.axis_size("quad"), lax.axis_size("tm")
    stride = frames // LOOP
    slots = 3 * pieces
    rows = -(-slots * tiles // 8) * 8
    listed = block_offset.shape
    hbm = pl.BlockSpec(memory_space=pltpu.HBM)
    vmem = pl.BlockSpec(memory_space=pltpu.VMEM)
    weights = pltpu.VMEM((width, width), jnp.bfloat16)
    attended = pl.pallas_call(
        functools.partial(kernel, pieces, frames, stride),
        out_shape=jax.ShapeDtypeStruct((width, tok), jnp.bfloat16),
        in_specs=[hbm] * 8,
        out_specs=vmem,
        scratch_shapes=[
            pltpu.VMEM((slots, width, tok), jnp.bfloat16),
            weights,
            weights,
            weights,
            pltpu.VMEM(listed, jnp.int32),
            pltpu.VMEM(listed, jnp.int32),
            pltpu.VMEM(listed, jnp.int32),
            pltpu.VMEM(live_blocks.shape, jnp.int32),
            pltpu.VMEM((HEADS, width, tok), jnp.bfloat16),
            pltpu.VMEM((rows, tok), jnp.float32),
            pltpu.VMEM((slots, HEADS, tok, tok), jnp.float32),
            pltpu.VMEM((HEADS, 8, tok), jnp.float32),
            pltpu.VMEM((slots, tiles, width, tok), jnp.bfloat16),
            pltpu.SemaphoreType.DMA((8,)),
            pltpu.SemaphoreType.DMA((slots - 1,)),
            pltpu.SemaphoreType.DMA((slots,)),
        ],
        compiler_params=pltpu.CompilerParams(
            collective_id=0, has_side_effects=True, vmem_limit_bytes=60 << 20
        ),
    )(features[0].T, w_query, w_key, w_value, block_offset, block_quad, block_tile, live_blocks)
    mixed = lax.dot_general(
        w_out, attended, (((0,), (0,)), ((), ())), preferred_element_type=jnp.float32
    )
    return mixed.astype(jnp.bfloat16).T[None]


def solution(mesh):
    listed = P("tm", "quad", None)
    return jax.shard_map(
        body,
        mesh=mesh,
        in_specs=(listed, P(), P(), P(), P(), listed, listed, listed, P("tm", "quad")),
        out_specs=listed,
        check_vma=False,
    )
```

time: 20.2 us -> 18.3 us (0.906)
  local copies, waits for them, and re-layouts: 2.01 us -> 0.01 us
  matrix products: 0.88 us -> 1.77 us
  Pallas kernels: 17 us -> 16.4 us
    unnamed x17 -> x2, local copies, waits for them, and re-layouts: 2.01 us -> 0.01 us
    dot_general x1, matrix products: 0.88 us -> 1.77 us  [body(): lax.dot_general(w_out, attended, (((0,), (0,)), ((), ())), preferred_elem...]
    pallas_call x1, Pallas kernels: 17 us -> 16.4 us  [body(): pl.pallas_call(functools.partial(kernel, pieces, frames, stride), out_sha...]
where the time goes in v2:
time: 18.3 us; the launch traced here: 18.2 us
  Pallas kernels  16.4 us (90%)
  matrix products  1.77 us (10%)
    pallas_call x1, Pallas kernels, body(): pl.pallas_call(functools.partial(kernel, pieces, frames, stride), out_sha...  16.4 us
    dot_general x1, matrix products, body(): lax.dot_general(w_out, attended, (((0,), (0,)), ((), ())), preferred_elem...  1.77 us

profile of v2, /device:TPU:0, one launch (start us, length us, event | category | flops | bytes accessed | tf_op | source)
XLA Modules:
  0.0 18.2 jit_solution(11560618614020381764)
XLA Ops:
  0.0 0.0 copy-start
  0.0 16.4 %shard_map.91 = bf16[192,256]{1,0:T(8,128)(2,1)} custom-call(bf16[192,256]{1,0:T(8,128)(2,1)} %bitcast.7, bf16[192,192]{1,0:T(8,128)(2,1)} %wq_ref.1, bf16[192,192]{1,0:T(8,128)(2,1)} %wk_ref.1, bf16[192,192]{1,0:T(8,128)(2,1)} %wv_ref.1, s32[1,2,24]{2,1,0:T(2,128)} %offset_ref.1, s32[1,2,24]{2,1,0:T(2,128)} %quad_ref.1, s32[1,2,24]{2,1,0:T(2,128)} %tile_ref.1, ...), custom_call_target="tpu_custom_call" | custom-call | tf_op jit(solution)/shard_map/pallas_call | solution.py:171
  16.4 0.0 copy-done
  16.4 1.8 %fusion = bf16[1,256,192]{1,2,0:T(8,128)(2,1)} fusion(bf16[192,256]{1,0:T(8,128)(2,1)} %shard_map.91, bf16[192,192]{1,0:T(8,128)(2,1)S(1)} %copy-done), kind=kOutput, calls=%fused_computation.1 | convolution fusion | flops 18923520 | bytes 270336 | tf_op jit(solution)/shard_map/dot_general | solution.py:198
Async XLA Ops:
  0.0 16.4 %copy-start = (bf16[192,192]{1,0:T(8,128)(2,1)S(1)}, bf16[192,192]{1,0:T(8,128)(2,1)}, u32[]{:S(2)}) copy-start(bf16[192,192]{1,0:T(8,128)(2,1)} %param.13) | copy-start | bytes 221188

commit v3 on v2

--- a/solution.py
+++ b/solution.py
@@ -28,9 +28,9 @@
 
 def kernel(
     pieces, frames, stride,
-    feat_ref, wq_ref, wk_ref, wv_ref, offset_ref, quad_ref, tile_ref, live_ref,
+    feat_ref, wq_ref, wk_ref, wv_ref, wo_ref, offset_ref, quad_ref, tile_ref, live_ref,
     out_ref,
-    window, wq, wk, wv, offset, quads, places, live,
+    window, wq, wk, wv, wo, attended, offset, quads, places, live,
     queries, times, scores, peak, values,
     load_sem, send_sem, recv_sem,
 ):
@@ -42,10 +42,17 @@
     near, far = 2 - 2 * lax.rem(frame, 2), 2 * lax.rem(frame, 2)
     own = pieces + quad
 
+    paired = pieces == 2 and stride == 1
+    across = 1 - quad
+    behind, beyond = (lax.rem(frame + (w - 1) * stride + frames, frames) for w in (near, far))
     peers = []
+    if paired:
+        peers.append(({"tm": frame, "quad": across}, own))
+        peers.append(({"tm": beyond, "quad": quad}, (2 - far) * pieces + quad))
+        peers.append(({"tm": behind, "quad": quad}, (2 - near) * pieces + quad))
     for rank, which in enumerate((far, 1, near)):
         for turn in range(pieces):
-            if rank == 1 and turn == 0:
+            if paired or (rank == 1 and turn == 0):
                 continue
             there = lax.rem(frame + (which - 1) * stride + frames, frames)
             slot = (2 - which) * pieces + quad
@@ -58,6 +65,7 @@
     pairs = (
         (wq_ref, wq), (feat_ref, window.at[own]), (wk_ref, wk), (wv_ref, wv),
         (offset_ref, offset), (quad_ref, quads), (tile_ref, places), (live_ref, live),
+        (wo_ref, wo),
     )
     loads = [
         pltpu.make_async_copy(source, target, load_sem.at[n])
@@ -67,17 +75,21 @@
         load.start()
     pl.semaphore_wait(barrier, len(peers))
     sends = []
-    for n, (device, slot) in enumerate(peers):
+
+    def launch(source, device, slot):
         send = pltpu.make_async_remote_copy(
-            src_ref=feat_ref,
+            src_ref=source,
             dst_ref=window.at[slot],
-            send_sem=send_sem.at[n],
+            send_sem=send_sem.at[len(sends)],
             recv_sem=recv_sem.at[slot],
             device_id=device,
             device_id_type=MESH,
         )
         send.start()
         sends.append(send)
+
+    for device, slot in peers:
+        launch(feat_ref, device, slot)
     for load in loads:
         load.wait()
 
@@ -120,15 +132,49 @@
 
     gather(own)
 
-    def arrive(step, carry):
-        turn = step // pieces
-        which = jnp.where(turn == 0, 1, jnp.where(turn == 1, near, far))
-        slot = which * pieces + lax.rem(quad + lax.rem(step, pieces), pieces)
+    def landed(slot):
         pltpu.make_async_copy(feat_ref, window.at[slot], recv_sem.at[slot]).wait()
-        gather(slot)
-        return carry
-
-    lax.fori_loop(1, slots, arrive, 0)
+
+    if paired:
+        facing, distant = pieces + across, far * pieces + quad
+        landed(facing)
+        launch(window.at[facing], {"tm": behind, "quad": quad}, (2 - near) * pieces + across)
+        landed(distant)
+        row = lax.rem(frame // 2 + lax.rem(frame, 2), 2)
+        launch(
+            window.at[jnp.where(row == 1, distant, facing)],
+            {
+                "tm": jnp.where(row == 1, frame, beyond),
+                "quad": jnp.where(row == 1, across, quad),
+            },
+            jnp.where(row == 1, distant, (2 - far) * pieces + across),
+        )
+        landed(near * pieces + quad)
+
+        def early(step, carry):
+            which = jnp.where(step == 0, 1, jnp.where(step == 1, near, far))
+            gather(which * pieces + jnp.where(step == 0, across, quad))
+            return carry
+
+        def late(step, carry):
+            slot = jnp.where(step == 0, near, far) * pieces + across
+            landed(slot)
+            gather(slot)
+            return carry
+
+        lax.fori_loop(0, 3, early, 0)
+        lax.fori_loop(0, 2, late, 0)
+    else:
+
+        def arrive(step, carry):
+            turn = step // pieces
+            which = jnp.where(turn == 0, 1, jnp.where(turn == 1, near, far))
+            slot = which * pieces + lax.rem(quad + lax.rem(step, pieces), pieces)
+            landed(slot)
+            gather(slot)
+            return carry
+
+        lax.fori_loop(1, slots, arrive, 0)
 
     for h in range(HEADS):
         top = jnp.max(peak[h], axis=0, keepdims=True)
@@ -150,7 +196,8 @@
             for j in range(tiles):
                 summed = summed + often[j] * o[j * head_dim : (j + 1) * head_dim]
         total = jnp.sum(total, axis=0, keepdims=True)
-        out_ref[span, :] = (summed / total).astype(jnp.bfloat16)
+        attended[span, :] = (summed / total).astype(jnp.bfloat16)
+    out_ref[...] = dot(wo[...].T, attended[...]).astype(jnp.bfloat16)
     for send in sends:
         send.wait_send()
 
@@ -168,16 +215,18 @@
     hbm = pl.BlockSpec(memory_space=pltpu.HBM)
     vmem = pl.BlockSpec(memory_space=pltpu.VMEM)
     weights = pltpu.VMEM((width, width), jnp.bfloat16)
-    attended = pl.pallas_call(
+    mixed = pl.pallas_call(
         functools.partial(kernel, pieces, frames, stride),
         out_shape=jax.ShapeDtypeStruct((width, tok), jnp.bfloat16),
-        in_specs=[hbm] * 8,
+        in_specs=[hbm] * 9,
         out_specs=vmem,
         scratch_shapes=[
             pltpu.VMEM((slots, width, tok), jnp.bfloat16),
             weights,
             weights,
             weights,
+            weights,
+            pltpu.VMEM((width, tok), jnp.bfloat16),
             pltpu.VMEM(listed, jnp.int32),
             pltpu.VMEM(listed, jnp.int32),
             pltpu.VMEM(listed, jnp.int32),
@@ -187,18 +236,15 @@
             pltpu.VMEM((slots, HEADS, tok, tok), jnp.float32),
             pltpu.VMEM((HEADS, 8, tok), jnp.float32),
             pltpu.VMEM((slots, tiles, width, tok), jnp.bfloat16),
-            pltpu.SemaphoreType.DMA((8,)),
+            pltpu.SemaphoreType.DMA((9,)),
             pltpu.SemaphoreType.DMA((slots - 1,)),
             pltpu.SemaphoreType.DMA((slots,)),
         ],
         compiler_params=pltpu.CompilerParams(
             collective_id=0, has_side_effects=True, vmem_limit_bytes=60 << 20
         ),
-    )(features[0].T, w_query, w_key, w_value, block_offset, block_quad, block_tile, live_blocks)
-    mixed = lax.dot_general(
-        w_out, attended, (((0,), (0,)), ((), ())), preferred_element_type=jnp.float32
-    )
-    return mixed.astype(jnp.bfloat16).T[None]
+    )(features[0].T, w_query, w_key, w_value, w_out, block_offset, block_quad, block_tile, live_blocks)
+    return mixed.T[None]
 
 
 def solution(mesh):

time: 18.3 us -> 19.8 us (1.082)
  matrix products: 1.77 us -> 0 us
  Pallas kernels: 16.4 us -> 18.1 us
  local copies, waits for them, and re-layouts: 0.01 us -> 1.54 us
    dot_general x1 -> x0, matrix products: 1.77 us -> none  [body(): lax.dot_general(w_out, attended, (((0,), (0,)), ((), ())), preferred_elem...]
    pallas_call x1, Pallas kernels: 16.4 us -> 18.1 us  [body(): pl.pallas_call(functools.partial(kernel, pieces, frames, stride), out_sha...]
    unnamed x2 -> x1, local copies, waits for them, and re-layouts: 0.01 us -> 1.54 us
where the time goes in v3:
time: 19.8 us; the launch traced here: 19.7 us
  Pallas kernels  18.1 us (91%)
  local copies, waits for them, and re-layouts  1.54 us (8%)
    pallas_call x1, Pallas kernels, body(): pl.pallas_call(functools.partial(kernel, pieces, frames, stride), out_sha...  18.1 us
    unnamed x1, local copies, waits for them, and re-layouts  1.54 us

profile of v3, /device:TPU:0, one launch (start us, length us, event | category | flops | bytes accessed | tf_op | source)
XLA Modules:
  0.0 19.7 jit_solution(156471610548562272)
XLA Ops:
  0.0 18.1 %shard_map.91 = bf16[192,256]{1,0:T(8,128)(2,1)} custom-call(bf16[192,256]{1,0:T(8,128)(2,1)} %bitcast.7, bf16[192,192]{1,0:T(8,128)(2,1)} %wq_ref.1, bf16[192,192]{1,0:T(8,128)(2,1)} %wk_ref.1, bf16[192,192]{1,0:T(8,128)(2,1)} %wv_ref.1, bf16[192,192]{1,0:T(8,128)(2,1)} %wo_ref.1, s32[1,2,24]{2,1,0:T(2,128)} %offset_ref.1, s32[1,2,24]{2,1,0:T(2,128)} %quad_ref.1, ...), custom_call_target="tpu_custom_call" | custom-call | tf_op jit(solution)/shard_map/pallas_call | solution.py:218
  18.1 1.5 %copy.11 = bf16[1,256,192]{1,2,0:T(8,128)(2,1)} copy(bf16[1,256,192]{1,2,0:T(8,128)(2,1)} %bitcast.6) | data formatting | bytes 196608

commit v4 on v2

--- a/solution.py
+++ b/solution.py
@@ -28,9 +28,9 @@
 
 def kernel(
     pieces, frames, stride,
-    feat_ref, wq_ref, wk_ref, wv_ref, offset_ref, quad_ref, tile_ref, live_ref,
+    feat_ref, wq_ref, wk_ref, wv_ref, wo_ref, offset_ref, quad_ref, tile_ref, live_ref,
     out_ref,
-    window, wq, wk, wv, offset, quads, places, live,
+    window, wq, wk, wv, wo, attended, offset, quads, places, live,
     queries, times, scores, peak, values,
     load_sem, send_sem, recv_sem,
 ):
@@ -58,6 +58,7 @@
     pairs = (
         (wq_ref, wq), (feat_ref, window.at[own]), (wk_ref, wk), (wv_ref, wv),
         (offset_ref, offset), (quad_ref, quads), (tile_ref, places), (live_ref, live),
+        (wo_ref, wo),
     )
     loads = [
         pltpu.make_async_copy(source, target, load_sem.at[n])
@@ -65,19 +66,6 @@
     ]
     for load in loads:
         load.start()
-    pl.semaphore_wait(barrier, len(peers))
-    sends = []
-    for n, (device, slot) in enumerate(peers):
-        send = pltpu.make_async_remote_copy(
-            src_ref=feat_ref,
-            dst_ref=window.at[slot],
-            send_sem=send_sem.at[n],
-            recv_sem=recv_sem.at[slot],
-            device_id=device,
-            device_id_type=MESH,
-        )
-        send.start()
-        sends.append(send)
     for load in loads:
         load.wait()
 
@@ -101,6 +89,20 @@
     for h in range(HEADS):
         queries[h] = jnp.where(head == h, query, jnp.zeros_like(query))
     key_tile = lanes(width, tok) // TILE
+
+    pl.semaphore_wait(barrier, len(peers))
+    sends = []
+    for n, (device, slot) in enumerate(peers):
+        send = pltpu.make_async_remote_copy(
+            src_ref=window.at[own],
+            dst_ref=window.at[slot],
+            send_sem=send_sem.at[n],
+            recv_sem=recv_sem.at[slot],
+            device_id=device,
+            device_id_type=MESH,
+        )
+        send.start()
+        sends.append(send)
 
     def gather(slot):
         x = window[slot]
@@ -150,7 +152,8 @@
             for j in range(tiles):
                 summed = summed + often[j] * o[j * head_dim : (j + 1) * head_dim]
         total = jnp.sum(total, axis=0, keepdims=True)
-        out_ref[span, :] = (summed / total).astype(jnp.bfloat16)
+        attended[span, :] = (summed / total).astype(jnp.bfloat16)
+    out_ref[...] = dot(wo[...].T, attended[...]).astype(jnp.bfloat16)
     for send in sends:
         send.wait_send()
 
@@ -168,16 +171,18 @@
     hbm = pl.BlockSpec(memory_space=pltpu.HBM)
     vmem = pl.BlockSpec(memory_space=pltpu.VMEM)
     weights = pltpu.VMEM((width, width), jnp.bfloat16)
-    attended = pl.pallas_call(
+    mixed = pl.pallas_call(
         functools.partial(kernel, pieces, frames, stride),
         out_shape=jax.ShapeDtypeStruct((width, tok), jnp.bfloat16),
-        in_specs=[hbm] * 8,
+        in_specs=[hbm] * 9,
         out_specs=vmem,
         scratch_shapes=[
             pltpu.VMEM((slots, width, tok), jnp.bfloat16),
             weights,
             weights,
             weights,
+            weights,
+            pltpu.VMEM((width, tok), jnp.bfloat16),
             pltpu.VMEM(listed, jnp.int32),
             pltpu.VMEM(listed, jnp.int32),
             pltpu.VMEM(listed, jnp.int32),
@@ -187,18 +192,15 @@
             pltpu.VMEM((slots, HEADS, tok, tok), jnp.float32),
             pltpu.VMEM((HEADS, 8, tok), jnp.float32),
             pltpu.VMEM((slots, tiles, width, tok), jnp.bfloat16),
-            pltpu.SemaphoreType.DMA((8,)),
+            pltpu.SemaphoreType.DMA((9,)),
             pltpu.SemaphoreType.DMA((slots - 1,)),
             pltpu.SemaphoreType.DMA((slots,)),
         ],
         compiler_params=pltpu.CompilerParams(
             collective_id=0, has_side_effects=True, vmem_limit_bytes=60 << 20
         ),
-    )(features[0].T, w_query, w_key, w_value, block_offset, block_quad, block_tile, live_blocks)
-    mixed = lax.dot_general(
-        w_out, attended, (((0,), (0,)), ((), ())), preferred_element_type=jnp.float32
-    )
-    return mixed.astype(jnp.bfloat16).T[None]
+    )(features[0].T, w_query, w_key, w_value, w_out, block_offset, block_quad, block_tile, live_blocks)
+    return mixed.T[None]
 
 
 def solution(mesh):

time: 18.3 us -> 17.7 us (0.967)
  the two profiles are of different devices: /device:TPU:0 before, /device:TPU:1 now
where the time goes in v4:
time: 17.7 us; the launch traced here: 17.5 us
  Pallas kernels  16 us (90%)
  local copies, waits for them, and re-layouts  1.54 us (9%)
    pallas_call x1, Pallas kernels, body(): pl.pallas_call(functools.partial(kernel, pieces, frames, stride), out_sha...  16 us
    unnamed x1, local copies, waits for them, and re-layouts  1.54 us

profile of v4, /device:TPU:1, one launch (start us, length us, event | category | flops | bytes accessed | tf_op | source)
XLA Modules:
  0.0 17.5 jit_solution(2714137792465730094)
XLA Ops:
  0.0 16.0 %shard_map.91 = bf16[192,256]{1,0:T(8,128)(2,1)} custom-call(bf16[192,256]{1,0:T(8,128)(2,1)} %bitcast.7, bf16[192,192]{1,0:T(8,128)(2,1)} %wq_ref.1, bf16[192,192]{1,0:T(8,128)(2,1)} %wk_ref.1, bf16[192,192]{1,0:T(8,128)(2,1)} %wv_ref.1, bf16[192,192]{1,0:T(8,128)(2,1)} %wo_ref.1, s32[1,2,24]{2,1,0:T(2,128)} %offset_ref.1, s32[1,2,24]{2,1,0:T(2,128)} %quad_ref.1, ...), custom_call_target="tpu_custom_call" | custom-call | tf_op jit(solution)/shard_map/pallas_call | solution.py:174
  16.0 1.5 %copy.11 = bf16[1,256,192]{1,2,0:T(8,128)(2,1)} copy(bf16[1,256,192]{1,2,0:T(8,128)(2,1)} %bitcast.6) | data formatting | bytes 196608

commit v5 on v2

--- a/solution.py
+++ b/solution.py
@@ -28,9 +28,9 @@
 
 def kernel(
     pieces, frames, stride,
-    feat_ref, wq_ref, wk_ref, wv_ref, offset_ref, quad_ref, tile_ref, live_ref,
+    feat_ref, wq_ref, wk_ref, wv_ref, wo_ref, offset_ref, quad_ref, tile_ref, live_ref,
     out_ref,
-    window, wq, wk, wv, offset, quads, places, live,
+    window, wq, wk, wv, wo, attended, offset, quads, places, live,
     queries, times, scores, peak, values,
     load_sem, send_sem, recv_sem,
 ):
@@ -58,6 +58,7 @@
     pairs = (
         (wq_ref, wq), (feat_ref, window.at[own]), (wk_ref, wk), (wv_ref, wv),
         (offset_ref, offset), (quad_ref, quads), (tile_ref, places), (live_ref, live),
+        (wo_ref, wo),
     )
     loads = [
         pltpu.make_async_copy(source, target, load_sem.at[n])
@@ -65,11 +66,12 @@
     ]
     for load in loads:
         load.start()
+    loads[1].wait()
     pl.semaphore_wait(barrier, len(peers))
     sends = []
     for n, (device, slot) in enumerate(peers):
         send = pltpu.make_async_remote_copy(
-            src_ref=feat_ref,
+            src_ref=window.at[own],
             dst_ref=window.at[slot],
             send_sem=send_sem.at[n],
             recv_sem=recv_sem.at[slot],
@@ -78,7 +80,7 @@
         )
         send.start()
         sends.append(send)
-    for load in loads:
+    for load in loads[:1] + loads[2:]:
         load.wait()
 
     rows = times.shape[0]
@@ -150,7 +152,8 @@
             for j in range(tiles):
                 summed = summed + often[j] * o[j * head_dim : (j + 1) * head_dim]
         total = jnp.sum(total, axis=0, keepdims=True)
-        out_ref[span, :] = (summed / total).astype(jnp.bfloat16)
+        attended[span, :] = (summed / total).astype(jnp.bfloat16)
+    out_ref[...] = dot(wo[...].T, attended[...]).astype(jnp.bfloat16)
     for send in sends:
         send.wait_send()
 
@@ -168,16 +171,18 @@
     hbm = pl.BlockSpec(memory_space=pltpu.HBM)
     vmem = pl.BlockSpec(memory_space=pltpu.VMEM)
     weights = pltpu.VMEM((width, width), jnp.bfloat16)
-    attended = pl.pallas_call(
+    mixed = pl.pallas_call(
         functools.partial(kernel, pieces, frames, stride),
         out_shape=jax.ShapeDtypeStruct((width, tok), jnp.bfloat16),
-        in_specs=[hbm] * 8,
+        in_specs=[hbm] * 9,
         out_specs=vmem,
         scratch_shapes=[
             pltpu.VMEM((slots, width, tok), jnp.bfloat16),
             weights,
             weights,
             weights,
+            weights,
+            pltpu.VMEM((width, tok), jnp.bfloat16),
             pltpu.VMEM(listed, jnp.int32),
             pltpu.VMEM(listed, jnp.int32),
             pltpu.VMEM(listed, jnp.int32),
@@ -187,18 +192,15 @@
             pltpu.VMEM((slots, HEADS, tok, tok), jnp.float32),
             pltpu.VMEM((HEADS, 8, tok), jnp.float32),
             pltpu.VMEM((slots, tiles, width, tok), jnp.bfloat16),
-            pltpu.SemaphoreType.DMA((8,)),
+            pltpu.SemaphoreType.DMA((9,)),
             pltpu.SemaphoreType.DMA((slots - 1,)),
             pltpu.SemaphoreType.DMA((slots,)),
         ],
         compiler_params=pltpu.CompilerParams(
             collective_id=0, has_side_effects=True, vmem_limit_bytes=60 << 20
         ),
-    )(features[0].T, w_query, w_key, w_value, block_offset, block_quad, block_tile, live_blocks)
-    mixed = lax.dot_general(
-        w_out, attended, (((0,), (0,)), ((), ())), preferred_element_type=jnp.float32
-    )
-    return mixed.astype(jnp.bfloat16).T[None]
+    )(features[0].T, w_query, w_key, w_value, w_out, block_offset, block_quad, block_tile, live_blocks)
+    return mixed.T[None]
 
 
 def solution(mesh):

time: 18.3 us -> 17.3 us (0.945)
  the two profiles are of different devices: /device:TPU:0 before, /device:TPU:1 now
where the time goes in v5:
time: 17.3 us; the launch traced here: 17.2 us
  Pallas kernels  15.6 us (90%)
  local copies, waits for them, and re-layouts  1.54 us (9%)
    pallas_call x1, Pallas kernels, body(): pl.pallas_call(functools.partial(kernel, pieces, frames, stride), out_sha...  15.6 us
    unnamed x1, local copies, waits for them, and re-layouts  1.54 us

profile of v5, /device:TPU:1, one launch (start us, length us, event | category | flops | bytes accessed | tf_op | source)
XLA Modules:
  0.0 17.2 jit_solution(6313224772417317693)
XLA Ops:
  0.0 15.6 %shard_map.91 = bf16[192,256]{1,0:T(8,128)(2,1)} custom-call(bf16[192,256]{1,0:T(8,128)(2,1)} %bitcast.7, bf16[192,192]{1,0:T(8,128)(2,1)} %wq_ref.1, bf16[192,192]{1,0:T(8,128)(2,1)} %wk_ref.1, bf16[192,192]{1,0:T(8,128)(2,1)} %wv_ref.1, bf16[192,192]{1,0:T(8,128)(2,1)} %wo_ref.1, s32[1,2,24]{2,1,0:T(2,128)} %offset_ref.1, s32[1,2,24]{2,1,0:T(2,128)} %quad_ref.1, ...), custom_call_target="tpu_custom_call" | custom-call | tf_op jit(solution)/shard_map/pallas_call | solution.py:174
  15.6 1.5 %copy.11 = bf16[1,256,192]{1,2,0:T(8,128)(2,1)} copy(bf16[1,256,192]{1,2,0:T(8,128)(2,1)} %bitcast.6) | data formatting | bytes 196608
